TPU v7x, 32 devices: a whole 2x2x4 slice. The times are simulated.
32 devices in a mesh: member: 4 (over z), patch: 4 (over y, x), level: 2 (over core).
Axes of the slice: x: 2, y: 2, z: 4, core: 2. Of those that a mesh axis runs over, the one named last changes fastest.
Arguments:
- ensemble: bfloat16 [256, 4, 4, 2, 12, 1024], P('member', 'patch', None, 'level'), may hold values from -6 to 6
- observations: float32 [4, 4, 2, 128], P('patch', 'member'), may hold values from -9 to 9
- precision: float32 [4, 4, 2, 128], P('patch', 'member'), may hold values from 0.25 to 4
- valid_count: int32 [4, 4, 2], P('patch', 'member'), may hold values from 16 to 128, as said below
- position: int32 [4, 4, 2, 128], P('patch', 'member'), may hold values from 0 to 12287
- level_kernel: float32 [2, 12], P('level'), may hold values from -4 to 4
- listed_blocks: int32 [4, 4, 8], P('patch', 'member'), may hold values from 0 to 17, as said below
Outputs:
- analysis: bfloat16 [256, 4, 4, 2, 12, 1024], P('member', 'patch', None, 'level')
Inputs may be any that keep to these rules, and one draw needn't show every extreme that they name: `valid_count`: the valid observations of a block are its first slots; some block is full and some holds 16. `listed_blocks`: the entries of one patch are distinct, include both of the patch's own blocks (candidates 8 and 9), and name only patches inside the grid.
All inputs are finite; a program needn't handle non-finite values.
Results may differ from a plain program's by a relative error of at most 0.0082.
Values may be sent and summed in bfloat16 or wider, within the bound.
A program may use at most 128 MiB of HBM per device.

v0:
```python
import jax
import jax.numpy as jnp
from jax import lax
from jax.sharding import PartitionSpec as P

VARIABLES = 12
COLUMNS = 1024
SLOTS = 128
OWN_BLOCKS = 2
LISTED = 8
SWEEPS = 6


exact_precision = lax.Precision.HIGHEST


def extended(cells, sides, width):
    for axis, dim in sides:
        count = lax.axis_size(axis)
        ends = count - 1
        head = lax.slice_in_dim(cells, 0, width, axis=dim)
        tail = lax.slice_in_dim(cells, cells.shape[dim] - width, cells.shape[dim], axis=dim)
        cells = jnp.concatenate(
            [
                lax.ppermute(tail, axis, [(i, (i + 1) % count) for i in range(ends)]),
                cells,
                lax.ppermute(head, axis, [((i + 1) % count, i) for i in range(ends)]),
            ],
            axis=dim,
        )
    return cells


def taper_of(listed):
    stepped = listed // OWN_BLOCKS
    moved = jnp.abs(stepped // 3 - 1) + jnp.abs(stepped % 3 - 1)
    return jnp.where(moved == 0, 1.0, jnp.where(moved == 1, 0.6, 0.35)).astype(jnp.float32)


def weights_for(candidates, pairs, listed):
    members = candidates.shape[0]
    candidate_count = candidates.shape[1]
    choose_iota = lax.broadcasted_iota(jnp.int32, (LISTED, candidate_count), 1)
    selector = listed[:, None] == choose_iota
    chosen = jnp.einsum(
        "kjs,lj->kls", candidates, selector.astype(jnp.bfloat16), preferred_element_type=jnp.float32
    )
    chosen = chosen.astype(jnp.bfloat16).reshape(members, LISTED * SLOTS)
    picked = jnp.einsum(
        "ajs,lj->als", pairs, selector.astype(jnp.float32), precision=exact_precision
    )
    tapering = taper_of(listed)
    widened = lax.optimization_barrier(chosen).astype(jnp.float32)
    centre = jnp.mean(widened, axis=0)
    obs_pert = (widened - centre).astype(jnp.bfloat16)
    weight = (picked[1] * tapering[:, None]).reshape(LISTED * SLOTS)
    innovation = picked[0].reshape(LISTED * SLOTS) - centre
    pert_wide = lax.optimization_barrier(obs_pert).astype(jnp.float32)
    scaled = (pert_wide * jnp.sqrt(weight)).astype(jnp.bfloat16)
    identity = jnp.eye(members, dtype=jnp.float32)
    system = lax.dot_general(
        scaled, scaled, (((1,), (1,)), ((), ())), preferred_element_type=jnp.float32
    )
    system = system + (members - 1) / 1.1 * identity
    scaling = jnp.sqrt(jnp.sum(system * system))
    iterate = system / scaling
    inverse_root = identity
    for iteration in range(SWEEPS):
        middle = 1.5 * identity - 0.5 * jnp.dot(inverse_root, iterate, precision=exact_precision)
        iterate = jnp.dot(iterate, middle, precision=exact_precision)
        inverse_root = jnp.dot(middle, inverse_root, precision=exact_precision)
    forcing = jnp.dot(pert_wide, weight * innovation, precision=exact_precision)
    inner = jnp.dot(inverse_root, forcing, precision=exact_precision)
    mean_weight = jnp.dot(inverse_root, inner, precision=exact_precision) / scaling
    return (jnp.sqrt((members - 1) / scaling) * inverse_root + mean_weight[:, None]).astype(
        jnp.bfloat16
    )


def apply_weights(weights, fields):
    field_mean = jnp.mean(fields, axis=0, dtype=jnp.float32)
    field_pert = (fields - field_mean).astype(jnp.bfloat16)
    updated = lax.dot_general(
        weights, field_pert, (((0,), (0,)), ((), ())), preferred_element_type=jnp.float32
    )
    return (updated + field_mean).astype(jnp.bfloat16)


def observe(shaped_fields, where_flat, kernel):
    patch_count = where_flat.shape[0]
    slot_count = where_flat.shape[1]
    column_of = where_flat % COLUMNS
    variable_of = where_flat // COLUMNS
    column_iota = lax.broadcasted_iota(jnp.int32, (patch_count, COLUMNS, slot_count), 1)
    column_hot = (column_of[:, None, :] == column_iota).astype(jnp.bfloat16)
    spread = jnp.einsum(
        "kpvq,pqo->kpvo", shaped_fields, column_hot, preferred_element_type=jnp.float32
    )
    variable_iota = lax.broadcasted_iota(jnp.int32, (patch_count, VARIABLES, slot_count), 1)
    variable_weight = jnp.where(
        variable_of[:, None, :] == variable_iota, kernel[None, :, None], 0.0
    )
    return jnp.sum(spread * variable_weight[None], axis=2)


def body(ensemble, observations, precision, valid_count, position, level_kernel, listed_blocks):
    kernel = level_kernel[0]
    local_members = ensemble.shape[0]
    row_patches = ensemble.shape[2]
    where_all = lax.all_gather(position, "member", axis=1, tiled=True)
    shaped_fields = ensemble.reshape(local_members, row_patches, VARIABLES, COLUMNS)
    level_term = observe(shaped_fields, where_all.reshape(row_patches, OWN_BLOCKS * SLOTS), kernel)
    summed = lax.psum(level_term, "level")
    equiv_local = summed.astype(jnp.bfloat16).reshape(
        local_members, 1, row_patches, OWN_BLOCKS, SLOTS
    )
    fields, equivalent = (
        lax.all_to_all(ensemble, "member", split_axis=2, concat_axis=0, tiled=True),
        lax.all_to_all(equiv_local, "member", split_axis=2, concat_axis=0, tiled=True),
    )
    members = equivalent.shape[0]
    own_patches = equivalent.shape[2]
    slot_index = lax.broadcasted_iota(jnp.int32, precision.shape, 3)
    precision_used = jnp.where(slot_index < valid_count[..., None], precision, 0.0)
    observation_pair = jnp.stack([observations, precision_used])
    equiv_near = extended(equivalent, (("member", 2), ("patch", 1)), 1)
    pairs_near = extended(observation_pair, (("member", 2), ("patch", 1)), 1)
    fields_flat = fields.reshape(members, own_patches, VARIABLES * COLUMNS)
    patch_slot = 0
    candidates = equiv_near.reshape(members, 9 * OWN_BLOCKS, SLOTS)
    pairs = pairs_near.reshape(2, 9 * OWN_BLOCKS, SLOTS)
    weight_list = [weights_for(candidates, pairs, listed_blocks[0, patch_slot])]
    all_weights = jnp.stack(weight_list)
    patch_slot = 0
    results = [apply_weights(all_weights[patch_slot], fields_flat[:, patch_slot])]
    analysed = jnp.stack(results, axis=1).reshape(members, 1, own_patches, 1, VARIABLES, COLUMNS)
    return lax.all_to_all(analysed, "member", split_axis=0, concat_axis=2, tiled=True)


def solution(mesh):
    placed = (
        P("member", "patch", None, "level", None, None),
        P("patch", "member", None, None),
        P("patch", "member", None, None),
        P("patch", "member", None),
        P("patch", "member", None, None),
        P("level", None),
        P("patch", "member", None),
    )
    return jax.shard_map(
        body,
        mesh=mesh,
        in_specs=placed,
        out_specs=P("member", "patch", None, "level", None, None),
        check_vma=False,
    )
```

profile of v0, /device:TPU:13, one launch (start us, length us, event | category | flops | bytes accessed | tf_op | source)
XLA Modules:
  0.0 533.2 jit_solution(13897730960973311223)
XLA Ops:
  0.0 6.4 %all_gather.3 = s32[1,4,2,128]{3,2,0,1:T(2,128)S(1)} all-gather(s32[1,1,2,128]{3,2,0,1:T(2,128)} %bitcast.163), channel_id=1, replica_groups=mesh['member'=4,'patch'=4,'level'=2] {'member'}, dimensions={1}, use_global_device_ids=true | all-gather | bytes 5120 | tf_op jit(solution)/shard_map/all_gather | solution.py:110
  6.4 0.7 fusion.29
  7.2 6.7 %fusion.6 = f32[64,4,256]{2,0,1:T(8,128)S(1)} fusion(f32[4,12,256]{2,1,0:T(8,128)S(1)} %fusion.29, bf16[64,4,12,1024]{3,1,2,0:T(4,128)(2,1)} %bitcast.147, s32[4,256]{1,0:T(4,128)S(1)} %get-tuple-element.8), kind=kOutput, calls=%fused_computation.10 | convolution fusion | flops 1613168640 | bytes 6606848 | tf_op jit(solution)/shard_map/kpvq,pqo->kpvo/dot_general | solution.py:96
  13.9 6.7 %all-reduce.1 = bf16[64,4,256]{2,0,1:T(8,128)(2,1)S(1)} all-reduce(f32[64,4,256]{2,0,1:T(8,128)S(1)} %fusion.6), channel_id=1, replica_groups=mesh['member'=4,'patch'=4,'level'=2] {'level'}, use_global_device_ids=true, to_apply=%region_1.2 | all-reduce | flops 65536 | bytes 393216 | tf_op jit(solution)/shard_map/psum | solution.py:113
  20.6 0.7 reshape.192
  21.3 6.4 %all-to-all-start = ((bf16[64,1,4,2,128]{4,3,0,1,2:T(2,128)(2,1)}), bf16[64,1,4,2,128]{4,3,0,1,2:T(2,128)(2,1)S(1)}, u32[]{:S(2)}, u32[]{:S(2)}) async-start(bf16[64,1,4,2,128]{4,3,0,1,2:T(2,128)(2,1)} %bitcast.8), calls=%async_computation | async-start | bytes 262144 | tf_op jit(solution)/shard_map/all_to_all | solution.py:119
  27.7 8.5 %copy.36 = bf16[64,1,4,1,12,1024]{5,4,3,1,0,2:T(8,128)(2,1)} copy(bf16[64,1,4,1,12,1024]{5,2,4,3,1,0:T(4,128)(2,1)} %param.7) | data formatting | bytes 12582912 | tf_op args[0]
  36.2 5.8 %all-to-all-start.1 = ((bf16[64,1,4,1,12,1024]{5,4,3,1,0,2:T(8,128)(2,1)}), bf16[64,1,4,1,12,1024]{5,4,3,1,0,2:T(8,128)(2,1)}, u32[]{:S(2)}, u32[]{:S(2)}) async-start(bf16[64,1,4,1,12,1024]{5,4,3,1,0,2:T(8,128)(2,1)} %copy.36), calls=%async_computation.1 | async-start | bytes 16777216 | tf_op jit(solution)/shard_map/all_to_all | solution.py:118
  42.1 2.0 collective-permute-start.1
  44.1 3.3 collective-permute-start
  47.4 2.0 collective-permute-start.5
  49.4 3.3 collective-permute-start.4
  52.7 174.0 %collective-permute-done.5 = f32[2,1,1,2,128]{4,3,2,1,0:T(2,128)S(1)} collective-permute-done((f32[2,1,1,2,128]{4,3,2,1,0:T(2,128)S(1)}, f32[2,1,1,2,128]{4,3,2,1,0:T(2,128)S(1)}, u32[]{:S(2)}, u32[]{:S(2)}) %collective-permute-start.5) | collective-permute-done | bytes 2080 | tf_op jit(solution)/shard_map/ppermute | solution.py:27
  226.7 3.1 collective-permute-start.7
  229.8 2.2 collective-permute-start.6
  232.1 4.0 collective-permute-start.3
  236.0 2.1 collective-permute-start.2
  238.4 4.6 collective-permute-done.3
  243.0 9.3 %collective-permute-done.2 = bf16[256,1,3,2,128]{4,0,3,2,1:T(8,128)(2,1)S(1)} collective-permute-done((bf16[256,1,3,2,128]{4,0,3,2,1:T(8,128)(2,1)S(1)}, bf16[256,1,3,2,128]{4,0,3,2,1:T(8,128)(2,1)S(1)}, u32[]{:S(2)}, u32[]{:S(2)}) %collective-permute-start.2) | collective-permute-done | bytes 393248 | tf_op jit(solution)/shard_map/ppermute | solution.py:25
  252.5 1.0 fusion.10
  253.9 0.9 multiply_reduce_fusion
  255.6 0.3 fusion.18
  256.2 0.5 convolution_bitcast_fusion.2
  256.7 0.4 fusion.28
  257.2 0.4 fusion.17
  257.5 0.4 fusion.47
  257.9 0.4 fusion.46
  258.3 0.4 fusion.16
  258.7 0.4 fusion.49
  259.1 0.4 fusion.48
  259.5 0.4 fusion.15
  259.9 0.4 fusion.51
  260.3 0.4 fusion.50
  260.6 0.4 fusion.14
  261.0 0.4 fusion.52
  261.4 0.4 fusion.53
  261.8 0.4 fusion.13
  262.2 0.4 fusion.54
  262.9 0.3 fusion.55
  263.3 5.1 convert_reduce_fusion
  268.4 11.6 %convert_element_type.69 = f32[64,1,4,1,12,1024]{5,4,3,1,0,2:T(8,128)} convert(bf16[64,1,4,1,12,1024]{5,4,3,1,0,2:T(8,128)(2,1)} %all-to-all-done.1) | non-fusion elementwise | flops 3145728 | bytes 18874368 | tf_op jit(solution)/shard_map/convert_element_type | solution.py:82
  280.0 23.2 %copy.44 = f32[32,8,12,1024]{3,1,2,0:T(8,128)} copy(f32[32,8,12,1024]{3,2,1,0:T(8,128)} %bitcast.142) | data formatting | bytes 25165824
  303.2 9.2 %fusion = bf16[256,12288]{1,0:T(8,128)(2,1)} fusion(f32[256,12288]{1,0:T(8,128)} %bitcast.143, f32[12288]{0:T(1024)S(1)} %div.76, f32[256,256]{1,0:T(8,128)S(1)} %fusion.54, f32[256]{0:T(256)S(1)} %broadcast_divide_fusion.3, f32[]{:T(128)S(6)} %sqrt.15), kind=kOutput, calls=%fused_computation.1 | convolution fusion | flops 1623392256 | bytes 19186692 | tf_op jit(solution)/shard_map/dot_general | solution.py:83
  312.4 8.6 %copy.37 = bf16[256,12288]{0,1:T(8,128)(2,1)} copy(bf16[256,12288]{1,0:T(8,128)(2,1)} %fusion) | data formatting | bytes 12582912 | tf_op jit(solution)/shard_map/convert_element_type | solution.py:86
  320.9 11.9 %copy.38 = bf16[256,1,1,1,12,1024]{5,4,3,2,1,0:T(8,128)(2,1)} copy(bf16[256,1,1,1,12,1024]{0,5,4,3,2,1:T(8,128)(2,1)} %bitcast.144) | data formatting | bytes 12582912 | tf_op jit(solution)/shard_map/reshape;stack | solution.py:136
  332.8 183.4 %all_to_all.45 = bf16[256,1,1,1,12,1024]{5,4,3,2,1,0:T(8,128)(2,1)S(1)} all-to-all(bf16[256,1,1,1,12,1024]{5,4,3,2,1,0:T(8,128)(2,1)} %copy.38), channel_id=1, replica_groups=mesh['member'=4,'patch'=4,'level'=2] {'member'}, dimensions={0} | all-to-all | bytes 12582912 | tf_op jit(solution)/shard_map/all_to_all | solution.py:137
  516.3 6.2 %copy.39 = bf16[256,1,1,1,12,1024]{5,0,4,3,2,1:T(8,128)(2,1)} copy(bf16[256,1,1,1,12,1024]{5,4,3,2,1,0:T(8,128)(2,1)S(1)} %all_to_all.45) | data formatting | bytes 12582912 | tf_op jit(solution)/shard_map/all_to_all | solution.py:137
  522.4 10.3 %copy.40 = bf16[64,1,4,1,12,1024]{5,2,4,3,1,0:T(4,128)(2,1)} copy(bf16[64,1,4,1,12,1024]{5,0,2,4,3,1:T(8,128)(2,1)} %bitcast.145) | data formatting | bytes 12582912 | tf_op jit(solution)/shard_map/all_to_all | solution.py:137
  (35 shorter events, 1.6 us)
Async XLA Ops:
  21.3 14.9 %all-to-all-start = ((bf16[64,1,4,2,128]{4,3,0,1,2:T(2,128)(2,1)}), bf16[64,1,4,2,128]{4,3,0,1,2:T(2,128)(2,1)S(1)}, u32[]{:S(2)}, u32[]{:S(2)}) async-start(bf16[64,1,4,2,128]{4,3,0,1,2:T(2,128)(2,1)} %bitcast.8), calls=%async_computation | async-start | bytes 262144 | tf_op jit(solution)/shard_map/all_to_all | solution.py:119
  36.2 5.8 %copy-start.1 = (f32[1,1,2,128]{3,2,1,0:T(2,128)S(1)}, f32[1,1,2,128]{3,2,1,0:T(2,128)}, u32[]{:S(2)}) copy-start(f32[1,1,2,128]{3,2,1,0:T(2,128)} %param.9) | copy-start | bytes 3076
  36.2 5.8 %copy-start.3 = (s32[1,1,2]{2,1,0:T(1,128)S(1)}, s32[1,1,2]{2,1,0:T(1,128)}, u32[]{:S(2)}) copy-start(s32[1,1,2]{2,1,0:T(1,128)} %param.10) | copy-start | bytes 28
  36.2 11.2 %copy-start = (f32[1,1,2,128]{3,2,1,0:T(2,128)S(1)}, f32[1,1,2,128]{3,2,1,0:T(2,128)}, u32[]{:S(2)}) copy-start(f32[1,1,2,128]{3,2,1,0:T(2,128)} %param.8) | copy-start | bytes 3076
  36.2 201.9 %copy-start.2 = (s32[1,1,8]{2,1,0:T(1,128)S(1)}, s32[1,1,8]{2,1,0:T(1,128)}, u32[]{:S(2)}) copy-start(s32[1,1,8]{2,1,0:T(1,128)} %param.13) | copy-start | bytes 100
  36.2 227.0 %all-to-all-start.1 = ((bf16[64,1,4,1,12,1024]{5,4,3,1,0,2:T(8,128)(2,1)}), bf16[64,1,4,1,12,1024]{5,4,3,1,0,2:T(8,128)(2,1)}, u32[]{:S(2)}, u32[]{:S(2)}) async-start(bf16[64,1,4,1,12,1024]{5,4,3,1,0,2:T(8,128)(2,1)} %copy.36), calls=%async_computation.1 | async-start | bytes 16777216 | tf_op jit(solution)/shard_map/all_to_all | solution.py:118
  42.1 189.9 %collective-permute-start.1 = (bf16[256,1,1,2,128]{4,0,3,2,1:T(8,128)(2,1)S(1)}, bf16[256,1,1,2,128]{4,0,3,2,1:T(8,128)(2,1)S(1)}, u32[]{:S(2)}, u32[]{:S(2)}) collective-permute-start(bf16[256,1,1,2,128]{4,0,3,2,1:T(8,128)(2,1)S(1)} %bitcast.151), channel_id=1, source_target_pairs={{8,0},{16,8},{24,16},{9,1},{17,9},{25,17},{10,2},{18,10},{26,18},{... | collective-permute-start | bytes 393224 | tf_op jit(solution)/shard_map/ppermute | solution.py:27
  44.1 187.9 %collective-permute-start = (bf16[256,1,1,2,128]{4,0,3,2,1:T(8,128)(2,1)S(1)}, bf16[256,1,1,2,128]{4,0,3,2,1:T(8,128)(2,1)S(1)}, u32[]{:S(2)}, u32[]{:S(2)}) collective-permute-start(bf16[256,1,1,2,128]{4,0,3,2,1:T(8,128)(2,1)S(1)} %bitcast.152), channel_id=1, source_target_pairs={{0,8},{8,16},{16,24},{1,9},{9,17},{17,25},{2,10},{10,18},{18,26},{... | collective-permute-start | bytes 393224 | tf_op jit(solution)/shard_map/ppermute | solution.py:25
  47.4 179.3 %collective-permute-start.5 = (f32[2,1,1,2,128]{4,3,2,1,0:T(2,128)S(1)}, f32[2,1,1,2,128]{4,3,2,1,0:T(2,128)S(1)}, u32[]{:S(2)}, u32[]{:S(2)}) collective-permute-start(f32[2,1,1,2,128]{4,3,2,1,0:T(2,128)S(1)} %pad_maximum_fusion.4), channel_id=1, source_target_pairs={{8,0},{16,8},{24,16},{9,1},{17,9},{25,17},{10,2},{18,10},{26,18},{... | collective-permute-start | bytes 6152 | tf_op jit(solution)/shard_map/ppermute | solution.py:27
  49.4 177.3 %collective-permute-start.4 = (f32[2,1,1,2,128]{4,3,2,1,0:T(2,128)S(1)}, f32[2,1,1,2,128]{4,3,2,1,0:T(2,128)S(1)}, u32[]{:S(2)}, u32[]{:S(2)}) collective-permute-start(f32[2,1,1,2,128]{4,3,2,1,0:T(2,128)S(1)} %pad_maximum_fusion.4), channel_id=1, source_target_pairs={{0,8},{8,16},{16,24},{1,9},{9,17},{17,25},{2,10},{10,18},{18,26},{... | collective-permute-start | bytes 6152 | tf_op jit(solution)/shard_map/ppermute | solution.py:25
  226.7 11.5 %collective-permute-start.7 = (f32[2,1,3,2,128]{4,3,2,1,0:T(2,128)S(1)}, f32[2,1,3,2,128]{4,3,2,1,0:T(2,128)S(1)}, u32[]{:S(2)}, u32[]{:S(2)}) collective-permute-start(f32[2,1,3,2,128]{4,3,2,1,0:T(2,128)S(1)} %pad_maximum_fusion.3), channel_id=1, source_target_pairs={{2,0},{4,2},{6,4},{3,1},{5,3},{7,5},{10,8},{12,10},{14,12},{11,9},... | collective-permute-start | bytes 18440 | tf_op jit(solution)/shard_map/ppermute | solution.py:27
  229.8 8.4 %collective-permute-start.6 = (f32[2,1,3,2,128]{4,3,2,1,0:T(2,128)S(1)}, f32[2,1,3,2,128]{4,3,2,1,0:T(2,128)S(1)}, u32[]{:S(2)}, u32[]{:S(2)}) collective-permute-start(f32[2,1,3,2,128]{4,3,2,1,0:T(2,128)S(1)} %pad_maximum_fusion.3), channel_id=1, source_target_pairs={{0,2},{2,4},{4,6},{1,3},{3,5},{5,7},{8,10},{10,12},{12,14},{9,11},... | collective-permute-start | bytes 18440 | tf_op jit(solution)/shard_map/ppermute | solution.py:25
  232.1 11.0 %collective-permute-start.3 = (bf16[256,1,3,2,128]{4,0,3,2,1:T(8,128)(2,1)S(1)}, bf16[256,1,3,2,128]{4,0,3,2,1:T(8,128)(2,1)S(1)}, u32[]{:S(2)}, u32[]{:S(2)}) collective-permute-start(bf16[256,1,3,2,128]{4,0,3,2,1:T(8,128)(2,1)S(1)} %pad_maximum_fusion.1), channel_id=1, source_target_pairs={{2,0},{4,2},{6,4},{3,1},{5,3},{7,5},{10,8},{12,10},{14,12},{11,9},... | collective-permute-start | bytes 1179656 | tf_op jit(solution)/shard_map/ppermute | solution.py:27
  236.0 16.3 %collective-permute-start.2 = (bf16[256,1,3,2,128]{4,0,3,2,1:T(8,128)(2,1)S(1)}, bf16[256,1,3,2,128]{4,0,3,2,1:T(8,128)(2,1)S(1)}, u32[]{:S(2)}, u32[]{:S(2)}) collective-permute-start(bf16[256,1,3,2,128]{4,0,3,2,1:T(8,128)(2,1)S(1)} %pad_maximum_fusion.1), channel_id=1, source_target_pairs={{0,2},{2,4},{4,6},{1,3},{3,5},{5,7},{8,10},{10,12},{12,14},{9,11},... | collective-permute-start | bytes 1179656 | tf_op jit(solution)/shard_map/ppermute | solution.py:25
where the time goes:
time: 543 us; the launch traced here: 533 us
  blocking collectives  197 us (36%)
  waiting for transfers between devices  188 us (35%)
  local copies, waits for them, and re-layouts  69.5 us (13%)
  starting transfers between devices  34.1 us (6%)
  matrix products  25.5 us (5%)
  other arithmetic  18 us (3%)
    all_to_all x1, blocking collectives, body(): lax.all_to_all(analysed, 'member', split_axis=0, concat_axis=2, tiled=True)  183 us
    ppermute x4, waiting for transfers between devices, extended(): lax.ppermute(head, axis, [((i + 1) % count, i) for i in range(ends)])  179 us
    unnamed x11, local copies, waits for them, and re-layouts  31.8 us
    all_to_all x2, local copies, waits for them, and re-layouts, body(): lax.all_to_all(analysed, 'member', split_axis=0, concat_axis=2, tiled=True)  16.5 us
    another operation x1, local copies, waits for them, and re-layouts, body(): jnp.stack(results, axis=1)  11.9 us
    convert_element_type x1, other arithmetic, apply_weights(): field_pert = (fields - field_mean).astype(jnp.bfloat16)  11.6 us
    ppermute x4, starting transfers between devices, extended(): lax.ppermute(head, axis, [((i + 1) % count, i) for i in range(ends)])  11 us
    ppermute x4, starting transfers between devices, extended(): lax.ppermute(tail, axis, [(i, (i + 1) % count) for i in range(ends)])  10.9 us
  transfers between devices with their start and end apart: 10, of which 4 were waited for; matrix products, arithmetic and copies ran while one was open for 4% of the time, Pallas kernels for 0%

commit v1 on v0

v1 whole, which is shorter than its diff:
```python
import functools

import jax
import jax.numpy as jnp
from jax import lax
from jax.experimental import pallas as pl
from jax.experimental.pallas import tpu as pltpu
from jax.sharding import PartitionSpec as P

VARIABLES = 12
COLUMNS = 1024
SLOTS = 128
OWN_BLOCKS = 2
LISTED = 8
SWEEPS = 6

MESH = pl.DeviceIdType.MESH
exact_precision = lax.Precision.HIGHEST


def observe(shaped_fields, where_flat, kernel):
    patch_count = where_flat.shape[0]
    slot_count = where_flat.shape[1]
    column_of = where_flat % COLUMNS
    variable_of = where_flat // COLUMNS
    column_iota = lax.broadcasted_iota(jnp.int32, (patch_count, COLUMNS, slot_count), 1)
    column_hot = (column_of[:, None, :] == column_iota).astype(jnp.bfloat16)
    spread = jnp.einsum(
        "kpvq,pqo->kpvo", shaped_fields, column_hot, preferred_element_type=jnp.float32
    )
    variable_iota = lax.broadcasted_iota(jnp.int32, (patch_count, VARIABLES, slot_count), 1)
    variable_weight = jnp.where(
        variable_of[:, None, :] == variable_iota, kernel[None, :, None], 0.0
    )
    return jnp.sum(spread * variable_weight[None], axis=2)


def wait_bytes(ref, sem):
    pltpu.make_async_copy(ref, ref, sem).wait()


def kernel(
    n,
    rows,
    listed_ref,
    fields_ref,
    equiv_ref,
    pairs_ref,
    out_ref,
    recv,
    done,
    near,
    near_pairs,
    scaled_ref,
    weights_ref,
    recv_sem,
    send_sem,
    back_sem,
    back_send_sem,
    near_sem,
    near_send_sem,
    pair_sem,
    pair_send_sem,
):
    me = lax.axis_index("member")
    row = lax.axis_index("patch")
    level = lax.axis_index("level")
    members = recv.shape[1] * recv.shape[2]

    def row_inside(step):
        return (row + step >= 0) & (row + step < rows)

    barrier = pltpu.get_barrier_semaphore()
    for step in (-1, 0, 1):

        @pl.when(row_inside(step))
        def _():
            def greet(other, carry):
                @pl.when((other != me) if step == 0 else (other >= 0))
                def _():
                    pl.semaphore_signal(
                        barrier, inc=1, device_id=(other, row + step, level), device_id_type=MESH
                    )

                return carry

            lax.fori_loop(0, n, greet, 0)

    row_count = 1 + jnp.where(row > 0, 1, 0) + jnp.where(row < rows - 1, 1, 0)
    pl.semaphore_wait(barrier, row_count * n - 1)

    for step in (-1, 0, 1):
        slot = 1 - step

        @pl.when(row_inside(step))
        def _():
            def send(shift, carry):
                other = lax.rem(me + shift, n)
                pltpu.make_async_remote_copy(
                    src_ref=equiv_ref.at[pl.ds(other, 3)],
                    dst_ref=near.at[slot, me],
                    send_sem=near_send_sem.at[slot],
                    recv_sem=near_sem.at[slot],
                    device_id=(other, row + step, level),
                    device_id_type=MESH,
                ).start()
                return carry

            lax.fori_loop(1 if step == 0 else 0, n, send, 0)

        @pl.when(jnp.logical_not(row_inside(step)))
        def _():
            near[1 + step] = jnp.zeros(near.shape[1:], near.dtype)

    pltpu.make_async_copy(equiv_ref.at[pl.ds(me, 3)], near.at[1, me], near_sem.at[1]).start()

    def pair_copy(step, shift):
        return pltpu.make_async_remote_copy(
            src_ref=pairs_ref,
            dst_ref=near_pairs.at[1 - step, 1 - shift],
            send_sem=pair_send_sem.at[1 - step, 1 - shift],
            recv_sem=pair_sem.at[1 - step, 1 - shift],
            device_id=(me + shift, row + step, level),
            device_id_type=MESH,
        )

    def pair_inside(step, shift):
        return row_inside(step) & (me + shift >= 0) & (me + shift < n)

    ring = [(a, b) for a in (-1, 0, 1) for b in (-1, 0, 1) if (a, b) != (0, 0)]
    for step, shift in ring:

        @pl.when(pair_inside(step, shift))
        def _():
            pair_copy(step, shift).start()

        @pl.when(jnp.logical_not(pair_inside(step, shift)))
        def _():
            near_pairs[1 + step, 1 + shift] = jnp.zeros(near_pairs.shape[2:], near_pairs.dtype)

    near_pairs[1, 1] = pairs_ref[...]

    def send_fields(v, carry):
        pltpu.make_async_copy(fields_ref.at[v, me], recv.at[v, me], recv_sem.at[v]).start()

        def send(shift, inner):
            other = lax.rem(me + shift, n)
            pltpu.make_async_remote_copy(
                src_ref=fields_ref.at[v, other],
                dst_ref=recv.at[v, me],
                send_sem=send_sem.at[v],
                recv_sem=recv_sem.at[v],
                device_id=(other, row, level),
                device_id_type=MESH,
            ).start()
            return inner

        return lax.fori_loop(1, n, send, carry)

    lax.fori_loop(0, VARIABLES, send_fields, 0)

    for step in (-1, 0, 1):

        @pl.when(row_inside(step))
        def _():
            wait_bytes(near.at[1 + step], near_sem.at[1 + step])

    for step, shift in ring:

        @pl.when(pair_inside(step, shift))
        def _():
            wait_bytes(near_pairs.at[1 + step, 1 + shift], pair_sem.at[1 + step, 1 + shift])

    def gather(entry, forcing):
        candidate = listed_ref[entry]
        place = candidate // OWN_BLOCKS
        block = candidate % OWN_BLOCKS
        down = place // 3
        across = place % 3
        moved = jnp.abs(down - 1) + jnp.abs(across - 1)
        taper = jnp.where(moved == 0, 1.0, jnp.where(moved == 1, 0.6, 0.35)).astype(jnp.float32)
        chosen = near[down, :, across, block].astype(jnp.float32).reshape(members, SLOTS)
        pairs = near_pairs[down, across]
        seen = jnp.where(block == 0, pairs[0:1], pairs[1:2])
        weight = jnp.where(block == 0, pairs[2:3], pairs[3:4]) * taper
        centre = jnp.sum(chosen, axis=0, keepdims=True) * (1.0 / members)
        pert = (chosen - centre).astype(jnp.bfloat16).astype(jnp.float32)
        scaled_ref[entry] = (pert * jnp.sqrt(weight)).astype(jnp.bfloat16)
        return forcing + jnp.sum(pert * (weight * (seen - centre)), axis=1, keepdims=True)

    forcing = lax.fori_loop(0, LISTED, gather, jnp.zeros((members, 1), jnp.float32))
    same = lax.broadcasted_iota(jnp.int32, (members, members), 0) == lax.broadcasted_iota(
        jnp.int32, (members, members), 1
    )
    identity = jnp.where(same, 1.0, 0.0).astype(jnp.float32)

    def outer(entry, system):
        part = scaled_ref[entry]
        return system + lax.dot_general(
            part, part, (((1,), (1,)), ((), ())), preferred_element_type=jnp.float32
        )

    system = lax.fori_loop(0, LISTED, outer, (members - 1) / 1.1 * identity)
    square = jnp.sum(jnp.sum(system * system, axis=1, keepdims=True), axis=0, keepdims=True)
    scaling = jnp.sqrt(square)

    def exact(a, b):
        return jnp.dot(a, b, precision=exact_precision, preferred_element_type=jnp.float32)

    def sweep(_, carry):
        iterate, inverse_root = carry
        middle = 1.5 * identity - 0.5 * exact(inverse_root, iterate)
        return exact(iterate, middle), exact(middle, inverse_root)

    _, inverse_root = lax.fori_loop(0, SWEEPS, sweep, (system / scaling, identity))
    wide = jnp.broadcast_to(forcing, (members, SLOTS))
    mean_weight = exact(inverse_root, exact(inverse_root, wide))[:, 0:1] / scaling
    weights = jnp.sqrt((members - 1) / scaling) * inverse_root + mean_weight
    weights_ref[...] = weights.T.astype(jnp.bfloat16)

    def apply(v, carry):
        wait_bytes(recv.at[v], recv_sem.at[v])
        fields = recv[v].astype(jnp.float32).reshape(members, COLUMNS)
        mean = jnp.sum(fields, axis=0, keepdims=True) * (1.0 / members)
        pert = (fields - mean).astype(jnp.bfloat16)
        updated = jnp.dot(weights_ref[...], pert, preferred_element_type=jnp.float32) + mean
        done[v] = updated.reshape(done.shape[1:]).astype(done.dtype)

        def send(shift, inner):
            other = lax.rem(me + shift, n)
            pltpu.make_async_remote_copy(
                src_ref=done.at[v, other],
                dst_ref=out_ref.at[v, me],
                send_sem=back_send_sem.at[v],
                recv_sem=back_sem.at[v],
                device_id=(other, row, level),
                device_id_type=MESH,
            ).start()
            return inner

        lax.fori_loop(1, n, send, 0)
        pltpu.make_async_copy(done.at[v, me], out_ref.at[v, me], back_sem.at[v]).start()
        return carry

    lax.fori_loop(0, VARIABLES, apply, 0)

    for step in (-1, 0, 1):

        @pl.when(row_inside(step))
        def _():
            count = n - 1 if step == 0 else n
            wait_bytes(near.at[1 - step, pl.ds(0, count)], near_send_sem.at[1 - step])

    for step, shift in ring:

        @pl.when(pair_inside(step, shift))
        def _():
            pair_copy(step, shift).wait_send()

    def finish(v, carry):
        wait_bytes(recv.at[v, pl.ds(0, n - 1)], send_sem.at[v])
        wait_bytes(done.at[v, pl.ds(0, n - 1)], back_send_sem.at[v])
        wait_bytes(done.at[v], back_sem.at[v])
        return carry

    lax.fori_loop(0, VARIABLES, finish, 0)


def body(ensemble, observations, precision, valid_count, position, level_kernel, listed_blocks):
    n = lax.axis_size("member")
    rows = lax.axis_size("patch")
    local_members = ensemble.shape[0]
    row_patches = ensemble.shape[2]
    members = local_members * n
    where_all = lax.all_gather(position, "member", axis=1, tiled=True)
    shaped_fields = ensemble.reshape(local_members, row_patches, VARIABLES, COLUMNS)
    level_term = observe(
        shaped_fields, where_all.reshape(row_patches, OWN_BLOCKS * SLOTS), level_kernel[0]
    )
    summed = lax.psum(level_term, "level")
    equiv = summed.astype(jnp.bfloat16).reshape(local_members, row_patches, OWN_BLOCKS, SLOTS)
    equiv = jnp.pad(equiv.transpose(1, 2, 0, 3), ((1, 1), (0, 0), (0, 0), (0, 0)))
    slot_index = lax.broadcasted_iota(jnp.int32, precision.shape, 3)
    precision_used = jnp.where(slot_index < valid_count[..., None], precision, 0.0)
    pairs = jnp.concatenate(
        [observations[0, 0], precision_used[0, 0], jnp.zeros((4, SLOTS), jnp.float32)]
    )
    fields = shaped_fields.transpose(2, 1, 0, 3)
    parts = (VARIABLES, n, local_members, COLUMNS)
    sem = pltpu.SemaphoreType.DMA
    result = pl.pallas_call(
        functools.partial(kernel, n, rows),
        out_shape=jax.ShapeDtypeStruct(parts, jnp.bfloat16),
        in_specs=[
            pl.BlockSpec(memory_space=pltpu.SMEM),
            pl.BlockSpec(memory_space=pl.ANY),
            pl.BlockSpec(memory_space=pltpu.VMEM),
            pl.BlockSpec(memory_space=pltpu.VMEM),
        ],
        out_specs=pl.BlockSpec(memory_space=pl.ANY),
        scratch_shapes=[
            pltpu.VMEM(parts, jnp.bfloat16),
            pltpu.VMEM(parts, jnp.bfloat16),
            pltpu.VMEM((3, n, 3, OWN_BLOCKS, local_members, SLOTS), jnp.bfloat16),
            pltpu.VMEM((3, 3, 8, SLOTS), jnp.float32),
            pltpu.VMEM((LISTED, members, SLOTS), jnp.bfloat16),
            pltpu.VMEM((members, members), jnp.bfloat16),
            sem((VARIABLES,)),
            sem((VARIABLES,)),
            sem((VARIABLES,)),
            sem((VARIABLES,)),
            sem((3,)),
            sem((3,)),
            sem((3, 3)),
            sem((3, 3)),
        ],
        compiler_params=pltpu.CompilerParams(
            collective_id=0, has_side_effects=True, vmem_limit_bytes=48 * 1024 * 1024
        ),
    )(listed_blocks[0, 0], fields, equiv, pairs)
    return result.transpose(2, 1, 0, 3).reshape(ensemble.shape)


def solution(mesh):
    placed = (
        P("member", "patch", None, "level", None, None),
        P("patch", "member", None, None),
        P("patch", "member", None, None),
        P("patch", "member", None),
        P("patch", "member", None, None),
        P("level", None),
        P("patch", "member", None),
    )
    return jax.shard_map(
        body,
        mesh=mesh,
        in_specs=placed,
        out_specs=P("member", "patch", None, "level", None, None),
        check_vma=False,
    )
```

time: 543 us -> 345 us (0.64); the launches traced: 533 us -> 344 us
  Pallas kernels: 0 us -> 303 us
  waiting for transfers between devices: 188 us -> 0 us
  blocking collectives: 197 us -> 13.1 us
  local copies, waits for them, and re-layouts: 69.5 us -> 19.5 us
  starting transfers between devices: 34.1 us -> 0 us
  matrix products: 25.5 us -> 6.7 us
  other arithmetic: 18 us -> 2.24 us
    pallas_call x0 -> x1, Pallas kernels: none -> 303 us  [body(): pl.pallas_call(functools.partial(kernel, n, rows), out_shape=jax.ShapeDty...]
    ppermute x8 -> x0, waiting for transfers between devices: 188 us -> none  [the longest x4 179 us: extended(): lax.ppermute(head, axis, [((i + 1) % count, i) for i in range(ends)])]
    all_to_all x1 -> x0, blocking collectives: 183 us -> none  [body(): lax.all_to_all(analysed, 'member', split_axis=0, concat_axis=2, tiled=True)]
    unnamed x11 -> x3, local copies, waits for them, and re-layouts: 31.8 us -> 8.99 us
    ppermute x8 -> x0, starting transfers between devices: 21.9 us -> none  [the longest x4 11 us: extended(): lax.ppermute(head, axis, [((i + 1) % count, i) for i in range(ends)])]
    dot_general x24 -> x0, matrix products: 18.8 us -> none  [the longest x1 9.21 us: apply_weights(): lax.dot_general(weights, field_pert, (((0,), (0,)), ((), ())), preferred_...]
    all_to_all x3 -> x0, local copies, waits for them, and re-layouts: 16.5 us -> none  [the longest x2 16.5 us: body(): lax.all_to_all(analysed, 'member', split_axis=0, concat_axis=2, tiled=True)]
    all_to_all x2 -> x0, starting transfers between devices: 12.2 us -> none  [the longest x1 6.42 us: body(): lax.all_to_all(equiv_local, 'member', split_axis=2, concat_axis=0, tiled=...]
  transfers between devices with their start and end apart: 10 -> 0, of which waited for: 4 -> 0; matrix products, arithmetic and copies ran while one was open for 4% -> 0% of each run, Pallas kernels for 0% -> 0%
where the time goes in v1:
time: 345 us; the launch traced here: 344 us
  Pallas kernels  303 us (88%)
  local copies, waits for them, and re-layouts  19.5 us (6%)
  blocking collectives  13.1 us (4%)
  matrix products  6.7 us (2%)
    pallas_call x1, Pallas kernels, body(): pl.pallas_call(functools.partial(kernel, n, rows), out_shape=jax.ShapeDty...  303 us
    reshape x1, local copies, waits for them, and re-layouts, body(): return result.transpose(2, 1, 0, 3).reshape(ensemble.shape)  10.3 us
    unnamed x3, local copies, waits for them, and re-layouts  8.99 us

profile of v1, /device:TPU:13, one launch (start us, length us, event | category | flops | bytes accessed | tf_op | source)
XLA Modules:
  0.0 344.5 jit_solution(13037184399786284439)
XLA Ops:
  0.0 0.1 pad.7.clone
  0.1 0.8 fusion.14
  0.8 0.7 maximum_maximum_fusion.pairs_ref
  1.6 6.4 %all_gather.3 = s32[1,4,2,128]{3,2,0,1:T(2,128)S(1)} all-gather(s32[1,1,2,128]{3,2,0,1:T(2,128)} %bitcast.69), channel_id=1, replica_groups=mesh['member'=4,'patch'=4,'level'=2] {'member'}, dimensions={1}, use_global_device_ids=true | all-gather | bytes 5120 | tf_op jit(solution)/shard_map/all_gather | solution.py:275
  8.0 0.7 fusion.11
  8.7 6.7 %fusion.5 = f32[64,4,256]{2,0,1:T(8,128)S(1)} fusion(f32[4,12,256]{2,1,0:T(8,128)S(1)} %fusion.11, bf16[64,1,4,1,12,1024]{5,2,4,3,1,0:T(4,128)(2,1)} %param.7, s32[4,256]{1,0:T(4,128)S(1)} %get-tuple-element.5), kind=kOutput, calls=%fused_computation.7 | convolution fusion | flops 1613168640 | bytes 6606848 | tf_op jit(solution)/shard_map/kpvq,pqo->kpvo/dot_general | solution.py:28
  15.4 6.7 %all-reduce.2 = bf16[64,4,256]{2,0,1:T(8,128)(2,1)S(1)} all-reduce(f32[64,4,256]{2,0,1:T(8,128)S(1)} %fusion.5), channel_id=1, replica_groups=mesh['member'=4,'patch'=4,'level'=2] {'level'}, use_global_device_ids=true, to_apply=%region_1.2 | all-reduce | flops 65536 | bytes 393216 | tf_op jit(solution)/shard_map/psum | solution.py:280
  22.2 0.0 copy-start
  22.2 9.0 %copy.47 = bf16[64,1,4,1,12,1024]{5,0,2,4,3,1:T(8,128)(2,1)} copy(bf16[64,1,4,1,12,1024]{5,2,4,3,1,0:T(4,128)(2,1)} %param.7) | data formatting | bytes 12582912 | tf_op args[0]
  31.2 0.0 copy-done
  31.2 302.9 %shard_map.76 = bf16[12,4,64,1024]{3,2,1,0:T(8,128)(2,1)} custom-call(s32[8]{0:T(128)S(1)} %bitcast.65, bf16[12,4,64,1024]{3,2,1,0:T(8,128)(2,1)} %bitcast.67, bf16[6,2,64,128]{3,2,1,0:T(8,128)(2,1)S(1)} %pad.4.equiv_ref, f32[8,128]{1,0:T(8,128)S(1)} %maximum_maximum_fusion.pairs_ref), custom_call_target="tpu_custom_call" | custom-call | tf_op jit(solution)/shard_map/pallas_call | solution.py:291
  334.1 10.3 %copy.19 = bf16[64,1,4,1,12,1024]{5,2,4,3,1,0:T(4,128)(2,1)} copy(bf16[64,1,4,1,12,1024]{5,0,2,4,3,1:T(8,128)(2,1)} %bitcast.66) | data formatting | bytes 12582912 | tf_op jit(solution)/shard_map/reshape | solution.py:321
  (4 shorter events, 0.1 us)
Async XLA Ops:
  22.2 9.0 %copy-start = (s32[1,1,8]{2,1,0:T(1,128)S(1)}, s32[1,1,8]{2,1,0:T(1,128)}, u32[]{:S(2)}) copy-start(s32[1,1,8]{2,1,0:T(1,128)} %param.13) | copy-start | bytes 100

commit v2 on v1

--- a/solution.py
+++ b/solution.py
@@ -18,23 +18,6 @@
 exact_precision = lax.Precision.HIGHEST
 
 
-def observe(shaped_fields, where_flat, kernel):
-    patch_count = where_flat.shape[0]
-    slot_count = where_flat.shape[1]
-    column_of = where_flat % COLUMNS
-    variable_of = where_flat // COLUMNS
-    column_iota = lax.broadcasted_iota(jnp.int32, (patch_count, COLUMNS, slot_count), 1)
-    column_hot = (column_of[:, None, :] == column_iota).astype(jnp.bfloat16)
-    spread = jnp.einsum(
-        "kpvq,pqo->kpvo", shaped_fields, column_hot, preferred_element_type=jnp.float32
-    )
-    variable_iota = lax.broadcasted_iota(jnp.int32, (patch_count, VARIABLES, slot_count), 1)
-    variable_weight = jnp.where(
-        variable_of[:, None, :] == variable_iota, kernel[None, :, None], 0.0
-    )
-    return jnp.sum(spread * variable_weight[None], axis=2)
-
-
 def wait_bytes(ref, sem):
     pltpu.make_async_copy(ref, ref, sem).wait()
 
@@ -42,33 +25,56 @@
 def kernel(
     n,
     rows,
+    lead,
     listed_ref,
+    valid_ref,
+    level_ref,
+    ensemble_ref,
+    position_ref,
+    observed_ref,
+    precision_ref,
+    out_ref,
+    loaded,
     fields_ref,
-    equiv_ref,
-    pairs_ref,
-    out_ref,
     recv,
     done,
+    where_ref,
+    term_ref,
+    other_term,
+    equiv_ref,
     near,
+    pairs_ref,
     near_pairs,
     scaled_ref,
     weights_ref,
+    load_sem,
     recv_sem,
     send_sem,
     back_sem,
     back_send_sem,
-    near_sem,
-    near_send_sem,
+    where_sem,
+    term_sem,
+    own_sem,
+    row_sem,
+    core_sem,
     pair_sem,
     pair_send_sem,
 ):
     me = lax.axis_index("member")
     row = lax.axis_index("patch")
     level = lax.axis_index("level")
-    members = recv.shape[1] * recv.shape[2]
+    local_members = recv.shape[2]
+    members = n * local_members
+    sibling = (me, row, 1 - level)
 
     def row_inside(step):
         return (row + step >= 0) & (row + step < rows)
+
+    def load(v, carry):
+        pltpu.make_async_copy(ensemble_ref.at[:, v], loaded.at[v], load_sem.at[v]).start()
+        return carry
+
+    lax.fori_loop(0, VARIABLES, load, 0)
 
     barrier = pltpu.get_barrier_semaphore()
     for step in (-1, 0, 1):
@@ -86,33 +92,32 @@
 
             lax.fori_loop(0, n, greet, 0)
 
+    pl.semaphore_signal(barrier, inc=1, device_id=sibling, device_id_type=MESH)
     row_count = 1 + jnp.where(row > 0, 1, 0) + jnp.where(row < rows - 1, 1, 0)
-    pl.semaphore_wait(barrier, row_count * n - 1)
-
-    for step in (-1, 0, 1):
-        slot = 1 - step
-
-        @pl.when(row_inside(step))
-        def _():
-            def send(shift, carry):
-                other = lax.rem(me + shift, n)
-                pltpu.make_async_remote_copy(
-                    src_ref=equiv_ref.at[pl.ds(other, 3)],
-                    dst_ref=near.at[slot, me],
-                    send_sem=near_send_sem.at[slot],
-                    recv_sem=near_sem.at[slot],
-                    device_id=(other, row + step, level),
-                    device_id_type=MESH,
-                ).start()
-                return carry
-
-            lax.fori_loop(1 if step == 0 else 0, n, send, 0)
-
-        @pl.when(jnp.logical_not(row_inside(step)))
-        def _():
-            near[1 + step] = jnp.zeros(near.shape[1:], near.dtype)
-
-    pltpu.make_async_copy(equiv_ref.at[pl.ds(me, 3)], near.at[1, me], near_sem.at[1]).start()
+    pl.semaphore_wait(barrier, row_count * n)
+
+    where_ref[me] = jnp.zeros(where_ref.shape[1:], where_ref.dtype)
+    where_ref[me, 0:OWN_BLOCKS] = position_ref[...]
+
+    def send_where(shift, carry):
+        pltpu.make_async_remote_copy(
+            src_ref=where_ref.at[me],
+            dst_ref=where_ref.at[me],
+            send_sem=where_sem.at[0],
+            recv_sem=where_sem.at[1],
+            device_id=(lax.rem(me + shift, n), row, level),
+            device_id_type=MESH,
+        ).start()
+        return carry
+
+    lax.fori_loop(1, n, send_where, 0)
+
+    slot_index = lax.broadcasted_iota(jnp.int32, (1, SLOTS), 1)
+    pairs_ref[...] = jnp.zeros(pairs_ref.shape, pairs_ref.dtype)
+    for block in range(OWN_BLOCKS):
+        pairs_ref[block] = observed_ref[block]
+        kept = jnp.where(slot_index < valid_ref[block], precision_ref[block : block + 1], 0.0)
+        pairs_ref[OWN_BLOCKS + block : OWN_BLOCKS + block + 1] = kept
 
     def pair_copy(step, shift):
         return pltpu.make_async_remote_copy(
@@ -140,9 +145,13 @@
 
     near_pairs[1, 1] = pairs_ref[...]
 
+    def arrange(v, carry):
+        wait_bytes(loaded.at[v], load_sem.at[v])
+        turned = jnp.transpose(loaded[v].astype(jnp.float32), (1, 0, 2))
+        fields_ref[v] = turned.astype(jnp.bfloat16)
+        return carry
+
     def send_fields(v, carry):
-        pltpu.make_async_copy(fields_ref.at[v, me], recv.at[v, me], recv_sem.at[v]).start()
-
         def send(shift, inner):
             other = lax.rem(me + shift, n)
             pltpu.make_async_remote_copy(
@@ -155,15 +164,115 @@
             ).start()
             return inner
 
-        return lax.fori_loop(1, n, send, carry)
-
-    lax.fori_loop(0, VARIABLES, send_fields, 0)
-
-    for step in (-1, 0, 1):
+        lax.fori_loop(1, n, send, 0)
+        pltpu.make_async_copy(fields_ref.at[v, me], recv.at[v, me], recv_sem.at[v]).start()
+        return carry
+
+    def arrange_and_send(v, carry):
+        return send_fields(v, arrange(v, carry))
+
+    lax.fori_loop(0, lead, arrange_and_send, 0)
+    lax.fori_loop(lead, VARIABLES, arrange, 0)
+
+    wait_bytes(where_ref.at[pl.ds(0, n - 1)], where_sem.at[1])
+    column_iota = lax.broadcasted_iota(jnp.int32, (COLUMNS, OWN_BLOCKS * SLOTS), 0)
+
+    def observe(p, carry):
+        where = where_ref[p]
+        where = jnp.concatenate([where[b : b + 1] for b in range(OWN_BLOCKS)], axis=1)
+        variable_of = where // COLUMNS
+        hot = jnp.where(where - variable_of * COLUMNS == column_iota, 1.0, 0.0)
+        fields = fields_ref[:, p]
+        if local_members % 16:
+            fields = fields.astype(jnp.float32)
+        fields = fields.reshape(VARIABLES * local_members, COLUMNS).astype(jnp.bfloat16)
+        spread = jnp.dot(fields, hot.astype(jnp.bfloat16), preferred_element_type=jnp.float32)
+        total = jnp.zeros((local_members, OWN_BLOCKS * SLOTS), jnp.float32)
+        for v in range(VARIABLES):
+            factor = jnp.where(variable_of == v, level_ref[v], 0.0)
+            total = total + spread[v * local_members : (v + 1) * local_members] * factor
+        for b in range(OWN_BLOCKS):
+            term_ref[b, p] = total[:, b * SLOTS : (b + 1) * SLOTS]
+        return carry
+
+    lax.fori_loop(0, n, observe, 0)
+    term_copy = pltpu.make_async_remote_copy(
+        src_ref=term_ref.at[1 - level],
+        dst_ref=other_term,
+        send_sem=term_sem.at[0],
+        recv_sem=term_sem.at[1],
+        device_id=sibling,
+        device_id_type=MESH,
+    )
+    term_copy.start()
+    lax.fori_loop(lead, lead + 1, send_fields, 0)
+    term_copy.wait_recv()
+    equiv_ref[0] = jnp.zeros(equiv_ref.shape[1:], equiv_ref.dtype)
+    equiv_ref[n + 1] = jnp.zeros(equiv_ref.shape[1:], equiv_ref.dtype)
+
+    def add_levels(p, carry):
+        equiv_ref[p + 1] = (term_ref[level, p] + other_term[p]).astype(jnp.bfloat16)
+        return carry
+
+    lax.fori_loop(0, n, add_levels, 0)
+
+    def send_own(shift, carry):
+        other = lax.rem(me + shift, n)
+        pltpu.make_async_remote_copy(
+            src_ref=equiv_ref.at[pl.ds(other, 3)],
+            dst_ref=near.at[level, 1, me],
+            send_sem=own_sem.at[0],
+            recv_sem=own_sem.at[1],
+            device_id=(other, row, level),
+            device_id_type=MESH,
+        ).start()
+        return carry
+
+    lax.fori_loop(1, n, send_own, 0)
+    pltpu.make_async_copy(
+        equiv_ref.at[pl.ds(me, 3)], near.at[level, 1, me], own_sem.at[1]
+    ).start()
+    lax.fori_loop(lead + 1, lead + 2, send_fields, 0)
+    wait_bytes(near.at[level, 1], own_sem.at[1])
+
+    def row_copy(step):
+        return pltpu.make_async_remote_copy(
+            src_ref=near.at[level, 1],
+            dst_ref=near.at[level, 1 - step],
+            send_sem=row_sem.at[0, 1 - step],
+            recv_sem=row_sem.at[1, 1 - step],
+            device_id=(me, row + step, level),
+            device_id_type=MESH,
+        )
+
+    for step in (-1, 1):
 
         @pl.when(row_inside(step))
         def _():
-            wait_bytes(near.at[1 + step], near_sem.at[1 + step])
+            row_copy(step).start()
+
+        @pl.when(jnp.logical_not(row_inside(step)))
+        def _():
+            near[level, 1 + step] = jnp.zeros(near.shape[2:], near.dtype)
+
+    lax.fori_loop(lead + 2, lead + 3, send_fields, 0)
+    for step in (-1, 1):
+
+        @pl.when(row_inside(step))
+        def _():
+            wait_bytes(near.at[level, 1 + step], row_sem.at[1, 1 + step])
+
+    core_copy = pltpu.make_async_remote_copy(
+        src_ref=near.at[level],
+        dst_ref=near.at[level],
+        send_sem=core_sem.at[0],
+        recv_sem=core_sem.at[1],
+        device_id=sibling,
+        device_id_type=MESH,
+    )
+    core_copy.start()
+    lax.fori_loop(lead + 3, VARIABLES, send_fields, 0)
+    wait_bytes(near.at[1 - level], core_sem.at[1])
 
     for step, shift in ring:
 
@@ -179,7 +288,7 @@
         across = place % 3
         moved = jnp.abs(down - 1) + jnp.abs(across - 1)
         taper = jnp.where(moved == 0, 1.0, jnp.where(moved == 1, 0.6, 0.35)).astype(jnp.float32)
-        chosen = near[down, :, across, block].astype(jnp.float32).reshape(members, SLOTS)
+        chosen = near[block, down, :, across].astype(jnp.float32).reshape(members, SLOTS)
         pairs = near_pairs[down, across]
         seen = jnp.where(block == 0, pairs[0:1], pairs[1:2])
         weight = jnp.where(block == 0, pairs[2:3], pairs[3:4]) * taper
@@ -244,13 +353,16 @@
 
     lax.fori_loop(0, VARIABLES, apply, 0)
 
-    for step in (-1, 0, 1):
+    wait_bytes(where_ref.at[pl.ds(0, n - 1)], where_sem.at[0])
+    term_copy.wait_send()
+    wait_bytes(near.at[0, 1, pl.ds(0, n - 1)], own_sem.at[0])
+    for step in (-1, 1):
 
         @pl.when(row_inside(step))
         def _():
-            count = n - 1 if step == 0 else n
-            wait_bytes(near.at[1 - step, pl.ds(0, count)], near_send_sem.at[1 - step])
-
+            row_copy(step).wait_send()
+
+    core_copy.wait_send()
     for step, shift in ring:
 
         @pl.when(pair_inside(step, shift))
@@ -270,38 +382,30 @@
     n = lax.axis_size("member")
     rows = lax.axis_size("patch")
     local_members = ensemble.shape[0]
-    row_patches = ensemble.shape[2]
     members = local_members * n
-    where_all = lax.all_gather(position, "member", axis=1, tiled=True)
-    shaped_fields = ensemble.reshape(local_members, row_patches, VARIABLES, COLUMNS)
-    level_term = observe(
-        shaped_fields, where_all.reshape(row_patches, OWN_BLOCKS * SLOTS), level_kernel[0]
-    )
-    summed = lax.psum(level_term, "level")
-    equiv = summed.astype(jnp.bfloat16).reshape(local_members, row_patches, OWN_BLOCKS, SLOTS)
-    equiv = jnp.pad(equiv.transpose(1, 2, 0, 3), ((1, 1), (0, 0), (0, 0), (0, 0)))
-    slot_index = lax.broadcasted_iota(jnp.int32, precision.shape, 3)
-    precision_used = jnp.where(slot_index < valid_count[..., None], precision, 0.0)
-    pairs = jnp.concatenate(
-        [observations[0, 0], precision_used[0, 0], jnp.zeros((4, SLOTS), jnp.float32)]
-    )
-    fields = shaped_fields.transpose(2, 1, 0, 3)
+    lead = 4
+    shaped = ensemble.reshape(local_members, n, VARIABLES, COLUMNS).transpose(0, 2, 1, 3)
     parts = (VARIABLES, n, local_members, COLUMNS)
     sem = pltpu.SemaphoreType.DMA
+    smem = pl.BlockSpec(memory_space=pltpu.SMEM)
+    vmem = pl.BlockSpec(memory_space=pltpu.VMEM)
+    whole = pl.BlockSpec(memory_space=pl.ANY)
     result = pl.pallas_call(
-        functools.partial(kernel, n, rows),
+        functools.partial(kernel, n, rows, lead),
         out_shape=jax.ShapeDtypeStruct(parts, jnp.bfloat16),
-        in_specs=[
-            pl.BlockSpec(memory_space=pltpu.SMEM),
-            pl.BlockSpec(memory_space=pl.ANY),
-            pl.BlockSpec(memory_space=pltpu.VMEM),
-            pl.BlockSpec(memory_space=pltpu.VMEM),
-        ],
-        out_specs=pl.BlockSpec(memory_space=pl.ANY),
+        in_specs=[smem, smem, smem, whole, vmem, vmem, vmem],
+        out_specs=whole,
         scratch_shapes=[
+            pltpu.VMEM((VARIABLES, local_members, n, COLUMNS), jnp.bfloat16),
             pltpu.VMEM(parts, jnp.bfloat16),
             pltpu.VMEM(parts, jnp.bfloat16),
-            pltpu.VMEM((3, n, 3, OWN_BLOCKS, local_members, SLOTS), jnp.bfloat16),
+            pltpu.VMEM(parts, jnp.bfloat16),
+            pltpu.VMEM((n, 8, SLOTS), jnp.int32),
+            pltpu.VMEM((OWN_BLOCKS, n, local_members, SLOTS), jnp.float32),
+            pltpu.VMEM((n, local_members, SLOTS), jnp.float32),
+            pltpu.VMEM((n + 2, local_members, SLOTS), jnp.bfloat16),
+            pltpu.VMEM((OWN_BLOCKS, 3, n, 3, local_members, SLOTS), jnp.bfloat16),
+            pltpu.VMEM((8, SLOTS), jnp.float32),
             pltpu.VMEM((3, 3, 8, SLOTS), jnp.float32),
             pltpu.VMEM((LISTED, members, SLOTS), jnp.bfloat16),
             pltpu.VMEM((members, members), jnp.bfloat16),
@@ -309,15 +413,27 @@
             sem((VARIABLES,)),
             sem((VARIABLES,)),
             sem((VARIABLES,)),
-            sem((3,)),
-            sem((3,)),
+            sem((VARIABLES,)),
+            sem((2,)),
+            sem((2,)),
+            sem((2,)),
+            sem((2, 3)),
+            sem((2,)),
             sem((3, 3)),
             sem((3, 3)),
         ],
         compiler_params=pltpu.CompilerParams(
-            collective_id=0, has_side_effects=True, vmem_limit_bytes=48 * 1024 * 1024
+            collective_id=0, has_side_effects=True, vmem_limit_bytes=56 * 1024 * 1024
         ),
-    )(listed_blocks[0, 0], fields, equiv, pairs)
+    )(
+        listed_blocks[0, 0],
+        valid_count[0, 0],
+        level_kernel[0],
+        shaped,
+        position[0, 0],
+        observations[0, 0],
+        precision[0, 0],
+    )
     return result.transpose(2, 1, 0, 3).reshape(ensemble.shape)
 
 

time: 345 us -> 292 us (0.85)
  Pallas kernels: 303 us -> 281 us
  blocking collectives: 13.1 us -> 0 us
  local copies, waits for them, and re-layouts: 19.5 us -> 10.3 us
  matrix products: 6.7 us -> 0 us
    pallas_call x1, Pallas kernels: 303 us -> 281 us  [body(): pl.pallas_call(functools.partial(kernel, n, rows, lead), out_shape=jax.Sh...]
    unnamed x3 -> x0, local copies, waits for them, and re-layouts: 8.99 us -> none
    psum x1 -> x0, blocking collectives: 6.71 us -> none  [body(): summed = lax.psum(level_term, 'level')]
    dot_general x1 -> x0, matrix products: 6.7 us -> none  [observe(): jnp.einsum('kpvq,pqo->kpvo', shaped_fields, column_hot, preferred_element...]
    all_gather x1 -> x0, blocking collectives: 6.41 us -> none  [body(): where_all = lax.all_gather(position, 'member', axis=1, tiled=True)]
where the time goes in v2:
time: 292 us; the launch traced here: 291 us
  Pallas kernels  281 us (96%)
  local copies, waits for them, and re-layouts  10.3 us (4%)
    pallas_call x1, Pallas kernels, body(): pl.pallas_call(functools.partial(kernel, n, rows, lead), out_shape=jax.Sh...  281 us
    reshape x1, local copies, waits for them, and re-layouts, body(): return result.transpose(2, 1, 0, 3).reshape(ensemble.shape)  10.3 us

profile of v2, /device:TPU:13, one launch (start us, length us, event | category | flops | bytes accessed | tf_op | source)
XLA Modules:
  0.0 291.4 jit_solution(10465533360875275685)
XLA Ops:
  0.0 281.1 %shard_map.73 = bf16[12,4,64,1024]{3,2,1,0:T(8,128)(2,1)} custom-call(s32[8]{0:T(128)} %bitcast.17, s32[2]{0:T(128)} %bitcast.18, f32[12]{0:T(128)} %bitcast.19, bf16[64,12,4,1024]{3,2,1,0:T(4,128)(2,1)} %bitcast.13, s32[2,128]{1,0:T(2,128)} %bitcast.14, f32[2,128]{1,0:T(2,128)} %bitcast.15, f32[2,128]{1,0:T(2,128)} %bitcast.16), custom_call_target="tpu_custom_call" | custom-call | tf_op jit(solution)/shard_map/pallas_call | solution.py:393
  281.1 10.3 %copy.8 = bf16[64,1,4,1,12,1024]{5,2,4,3,1,0:T(4,128)(2,1)} copy(bf16[64,1,4,1,12,1024]{5,0,2,4,3,1:T(8,128)(2,1)} %bitcast.12) | data formatting | bytes 12582912 | tf_op jit(solution)/shard_map/reshape | solution.py:437

commit v3 on v2

--- a/solution.py
+++ b/solution.py
@@ -34,6 +34,7 @@
     observed_ref,
     precision_ref,
     out_ref,
+    landed,
     loaded,
     fields_ref,
     recv,
@@ -93,6 +94,14 @@
             lax.fori_loop(0, n, greet, 0)
 
     pl.semaphore_signal(barrier, inc=1, device_id=sibling, device_id_type=MESH)
+
+    def arrange(v, carry):
+        wait_bytes(loaded.at[v], load_sem.at[v])
+        turned = jnp.transpose(loaded[v].astype(jnp.float32), (1, 0, 2))
+        fields_ref[v] = turned.astype(jnp.bfloat16)
+        return carry
+
+    arrange(0, 0)
     row_count = 1 + jnp.where(row > 0, 1, 0) + jnp.where(row < rows - 1, 1, 0)
     pl.semaphore_wait(barrier, row_count * n)
 
@@ -111,45 +120,6 @@
         return carry
 
     lax.fori_loop(1, n, send_where, 0)
-
-    slot_index = lax.broadcasted_iota(jnp.int32, (1, SLOTS), 1)
-    pairs_ref[...] = jnp.zeros(pairs_ref.shape, pairs_ref.dtype)
-    for block in range(OWN_BLOCKS):
-        pairs_ref[block] = observed_ref[block]
-        kept = jnp.where(slot_index < valid_ref[block], precision_ref[block : block + 1], 0.0)
-        pairs_ref[OWN_BLOCKS + block : OWN_BLOCKS + block + 1] = kept
-
-    def pair_copy(step, shift):
-        return pltpu.make_async_remote_copy(
-            src_ref=pairs_ref,
-            dst_ref=near_pairs.at[1 - step, 1 - shift],
-            send_sem=pair_send_sem.at[1 - step, 1 - shift],
-            recv_sem=pair_sem.at[1 - step, 1 - shift],
-            device_id=(me + shift, row + step, level),
-            device_id_type=MESH,
-        )
-
-    def pair_inside(step, shift):
-        return row_inside(step) & (me + shift >= 0) & (me + shift < n)
-
-    ring = [(a, b) for a in (-1, 0, 1) for b in (-1, 0, 1) if (a, b) != (0, 0)]
-    for step, shift in ring:
-
-        @pl.when(pair_inside(step, shift))
-        def _():
-            pair_copy(step, shift).start()
-
-        @pl.when(jnp.logical_not(pair_inside(step, shift)))
-        def _():
-            near_pairs[1 + step, 1 + shift] = jnp.zeros(near_pairs.shape[2:], near_pairs.dtype)
-
-    near_pairs[1, 1] = pairs_ref[...]
-
-    def arrange(v, carry):
-        wait_bytes(loaded.at[v], load_sem.at[v])
-        turned = jnp.transpose(loaded[v].astype(jnp.float32), (1, 0, 2))
-        fields_ref[v] = turned.astype(jnp.bfloat16)
-        return carry
 
     def send_fields(v, carry):
         def send(shift, inner):
@@ -168,10 +138,45 @@
         pltpu.make_async_copy(fields_ref.at[v, me], recv.at[v, me], recv_sem.at[v]).start()
         return carry
 
+    send_fields(0, 0)
+
+    slot_index = lax.broadcasted_iota(jnp.int32, (1, SLOTS), 1)
+    pairs_ref[...] = jnp.zeros(pairs_ref.shape, pairs_ref.dtype)
+    for block in range(OWN_BLOCKS):
+        pairs_ref[block] = observed_ref[block]
+        kept = jnp.where(slot_index < valid_ref[block], precision_ref[block : block + 1], 0.0)
+        pairs_ref[OWN_BLOCKS + block : OWN_BLOCKS + block + 1] = kept
+
+    def pair_copy(step, shift):
+        return pltpu.make_async_remote_copy(
+            src_ref=pairs_ref,
+            dst_ref=near_pairs.at[1 - step, 1 - shift],
+            send_sem=pair_send_sem.at[1 - step, 1 - shift],
+            recv_sem=pair_sem.at[1 - step, 1 - shift],
+            device_id=(me + shift, row + step, level),
+            device_id_type=MESH,
+        )
+
+    def pair_inside(step, shift):
+        return row_inside(step) & (me + shift >= 0) & (me + shift < n)
+
+    ring = [(a, b) for a in (-1, 0, 1) for b in (-1, 0, 1) if (a, b) != (0, 0)]
+    for step, shift in ring:
+
+        @pl.when(pair_inside(step, shift))
+        def _():
+            pair_copy(step, shift).start()
+
+        @pl.when(jnp.logical_not(pair_inside(step, shift)))
+        def _():
+            near_pairs[1 + step, 1 + shift] = jnp.zeros(near_pairs.shape[2:], near_pairs.dtype)
+
+    near_pairs[1, 1] = pairs_ref[...]
+
     def arrange_and_send(v, carry):
         return send_fields(v, arrange(v, carry))
 
-    lax.fori_loop(0, lead, arrange_and_send, 0)
+    lax.fori_loop(1, lead, arrange_and_send, 0)
     lax.fori_loop(lead, VARIABLES, arrange, 0)
 
     wait_bytes(where_ref.at[pl.ds(0, n - 1)], where_sem.at[1])
@@ -339,7 +344,7 @@
             other = lax.rem(me + shift, n)
             pltpu.make_async_remote_copy(
                 src_ref=done.at[v, other],
-                dst_ref=out_ref.at[v, me],
+                dst_ref=landed.at[v, me],
                 send_sem=back_send_sem.at[v],
                 recv_sem=back_sem.at[v],
                 device_id=(other, row, level),
@@ -348,11 +353,20 @@
             return inner
 
         lax.fori_loop(1, n, send, 0)
-        pltpu.make_async_copy(done.at[v, me], out_ref.at[v, me], back_sem.at[v]).start()
+        pltpu.make_async_copy(done.at[v, me], landed.at[v, me], back_sem.at[v]).start()
         return carry
 
     lax.fori_loop(0, VARIABLES, apply, 0)
 
+    def restore(v, carry):
+        wait_bytes(landed.at[v], back_sem.at[v])
+        turned = jnp.transpose(landed[v].astype(jnp.float32), (1, 0, 2))
+        loaded[v] = turned.astype(jnp.bfloat16)
+        pltpu.make_async_copy(loaded.at[v], out_ref.at[:, v], load_sem.at[v]).start()
+        return carry
+
+
+    lax.fori_loop(0, VARIABLES, restore, 0)
     wait_bytes(where_ref.at[pl.ds(0, n - 1)], where_sem.at[0])
     term_copy.wait_send()
     wait_bytes(near.at[0, 1, pl.ds(0, n - 1)], own_sem.at[0])
@@ -372,7 +386,7 @@
     def finish(v, carry):
         wait_bytes(recv.at[v, pl.ds(0, n - 1)], send_sem.at[v])
         wait_bytes(done.at[v, pl.ds(0, n - 1)], back_send_sem.at[v])
-        wait_bytes(done.at[v], back_sem.at[v])
+        wait_bytes(loaded.at[v], load_sem.at[v])
         return carry
 
     lax.fori_loop(0, VARIABLES, finish, 0)
@@ -392,10 +406,11 @@
     whole = pl.BlockSpec(memory_space=pl.ANY)
     result = pl.pallas_call(
         functools.partial(kernel, n, rows, lead),
-        out_shape=jax.ShapeDtypeStruct(parts, jnp.bfloat16),
+        out_shape=jax.ShapeDtypeStruct(shaped.shape, jnp.bfloat16),
         in_specs=[smem, smem, smem, whole, vmem, vmem, vmem],
         out_specs=whole,
         scratch_shapes=[
+            pltpu.VMEM(parts, jnp.bfloat16),
             pltpu.VMEM((VARIABLES, local_members, n, COLUMNS), jnp.bfloat16),
             pltpu.VMEM(parts, jnp.bfloat16),
             pltpu.VMEM(parts, jnp.bfloat16),
@@ -434,7 +449,7 @@
         observations[0, 0],
         precision[0, 0],
     )
-    return result.transpose(2, 1, 0, 3).reshape(ensemble.shape)
+    return result.transpose(0, 2, 1, 3).reshape(ensemble.shape)
 
 
 def solution(mesh):

time: 292 us -> 293 us (level)
    reshape x1 -> x0, local copies, waits for them, and re-layouts: 10.3 us -> none  [body(): return result.transpose(2, 1, 0, 3).reshape(ensemble.shape)]
    unnamed x0 -> x1, local copies, waits for them, and re-layouts: none -> 10.1 us
where the time goes in v3:
time: 293 us; the launch traced here: 292 us
  Pallas kernels  282 us (96%)
  local copies, waits for them, and re-layouts  10.1 us (3%)
    pallas_call x1, Pallas kernels, body(): pl.pallas_call(functools.partial(kernel, n, rows, lead), out_shape=jax.Sh...  282 us
    unnamed x1, local copies, waits for them, and re-layouts  10.1 us

profile of v3, /device:TPU:13, one launch (start us, length us, event | category | flops | bytes accessed | tf_op | source)
XLA Modules:
  0.0 292.4 jit_solution(12304727170786858528)
XLA Ops:
  0.0 282.3 %shard_map.73 = bf16[64,12,4,1024]{3,2,1,0:T(4,128)(2,1)} custom-call(s32[8]{0:T(128)} %bitcast.19, s32[2]{0:T(128)} %bitcast.20, f32[12]{0:T(128)} %bitcast.21, bf16[64,12,4,1024]{3,2,1,0:T(4,128)(2,1)} %bitcast.15, s32[2,128]{1,0:T(2,128)} %bitcast.16, f32[2,128]{1,0:T(2,128)} %bitcast.17, f32[2,128]{1,0:T(2,128)} %bitcast.18), custom_call_target="tpu_custom_call" | custom-call | tf_op jit(solution)/shard_map/pallas_call | solution.py:407
  282.3 10.1 %copy.10 = bf16[64,1,4,1,12,1024]{5,2,4,3,1,0:T(4,128)(2,1)} copy(bf16[64,1,4,1,12,1024]{5,2,4,3,1,0:T(4,128)(2,1)} %bitcast.14) | data formatting | bytes 12582912

commit v4 on v3

--- a/solution.py
+++ b/solution.py
@@ -321,12 +321,31 @@
     def exact(a, b):
         return jnp.dot(a, b, precision=exact_precision, preferred_element_type=jnp.float32)
 
+    def halves(a):
+        high = a.astype(jnp.bfloat16)
+        return high, (a - high.astype(jnp.float32)).astype(jnp.bfloat16)
+
+    def product(a, b):
+        (a_high, a_low), (b_high, b_low) = a, b
+        return jnp.dot(
+            jnp.concatenate([a_low, a_high, a_high], axis=1),
+            jnp.concatenate([b_high, b_low, b_high], axis=0),
+            preferred_element_type=jnp.float32,
+        )
+
     def sweep(_, carry):
         iterate, inverse_root = carry
-        middle = 1.5 * identity - 0.5 * exact(inverse_root, iterate)
-        return exact(iterate, middle), exact(middle, inverse_root)
-
-    _, inverse_root = lax.fori_loop(0, SWEEPS, sweep, (system / scaling, identity))
+        iterate_parts, root_parts = halves(iterate), halves(inverse_root)
+        middle = halves(1.5 * identity - 0.5 * product(root_parts, iterate_parts))
+        return product(iterate_parts, middle), product(middle, root_parts)
+
+    iterate = system / scaling
+    inverse_root = 1.5 * identity - 0.5 * iterate
+    iterate = product(halves(iterate), halves(inverse_root))
+    iterate, inverse_root = lax.fori_loop(1, SWEEPS - 1, sweep, (iterate, inverse_root))
+    root_parts = halves(inverse_root)
+    middle = 1.5 * identity - 0.5 * product(root_parts, halves(iterate))
+    inverse_root = product(halves(middle), root_parts)
     wide = jnp.broadcast_to(forcing, (members, SLOTS))
     mean_weight = exact(inverse_root, exact(inverse_root, wide))[:, 0:1] / scaling
     weights = jnp.sqrt((members - 1) / scaling) * inverse_root + mean_weight
@@ -390,6 +409,16 @@
         return carry
 
     lax.fori_loop(0, VARIABLES, finish, 0)
+
+
+def hand_over(result_ref, out_ref, sem):
+    def piece(v):
+        return pltpu.make_async_copy(result_ref.at[:, v], out_ref.at[:, v], sem.at[v])
+
+    for v in range(VARIABLES):
+        piece(v).start()
+    for v in range(VARIABLES):
+        piece(v).wait()
 
 
 def body(ensemble, observations, precision, valid_count, position, level_kernel, listed_blocks):
@@ -449,6 +478,14 @@
         observations[0, 0],
         precision[0, 0],
     )
+    result = pl.pallas_call(
+        hand_over,
+        out_shape=jax.ShapeDtypeStruct(shaped.shape, jnp.bfloat16),
+        in_specs=[whole],
+        out_specs=whole,
+        scratch_shapes=[sem((VARIABLES,))],
+        compiler_params=pltpu.CompilerParams(vmem_limit_bytes=56 * 1024 * 1024),
+    )(result)
     return result.transpose(0, 2, 1, 3).reshape(ensemble.shape)
 
 

time: 293 us -> 474 us (1.62)
  Pallas kernels: 282 us -> 474 us
  local copies, waits for them, and re-layouts: 10.1 us -> 0 us
    pallas_call x0 -> x1, Pallas kernels: none -> 192 us  [body(): pl.pallas_call(hand_over, out_shape=jax.ShapeDtypeStruct(shaped.shape, jn...]
    unnamed x1 -> x0, local copies, waits for them, and re-layouts: 10.1 us -> none
where the time goes in v4:
time: 474 us
  Pallas kernels  474 us (100%)
    pallas_call x1, Pallas kernels, body(): pl.pallas_call(functools.partial(kernel, n, rows, lead), out_shape=jax.Sh...  282 us
    pallas_call x1, Pallas kernels, body(): pl.pallas_call(hand_over, out_shape=jax.ShapeDtypeStruct(shaped.shape, jn...  192 us

profile of v4, /device:TPU:13, one launch (start us, length us, event | category | flops | bytes accessed | tf_op | source)
XLA Modules:
  0.0 474.1 jit_solution(8607360752642317615)
XLA Ops:
  0.0 282.3 %shard_map.73.result_ref = bf16[64,12,4,1024]{3,2,1,0:T(4,128)(2,1)} custom-call(s32[8]{0:T(128)} %bitcast.18, s32[2]{0:T(128)} %bitcast.19, f32[12]{0:T(128)} %bitcast.20, bf16[64,12,4,1024]{3,2,1,0:T(4,128)(2,1)} %bitcast.14, s32[2,128]{1,0:T(2,128)} %bitcast.15, f32[2,128]{1,0:T(2,128)} %bitcast.16, f32[2,128]{1,0:T(2,128)} %bitcast.17), custom_call_target="tpu_custom_call" | custom-call | tf_op jit(solution)/shard_map/pallas_call | solution.py:436
  282.3 191.8 %shard_map.74 = bf16[64,12,4,1024]{3,2,1,0:T(4,128)(2,1)} custom-call(bf16[64,12,4,1024]{3,2,1,0:T(4,128)(2,1)} %shard_map.73.result_ref), custom_call_target="tpu_custom_call" | custom-call | tf_op jit(solution)/shard_map/pallas_call | solution.py:481

commit v5 on v4

--- a/solution.py
+++ b/solution.py
@@ -380,8 +380,7 @@
     def restore(v, carry):
         wait_bytes(landed.at[v], back_sem.at[v])
         turned = jnp.transpose(landed[v].astype(jnp.float32), (1, 0, 2))
-        loaded[v] = turned.astype(jnp.bfloat16)
-        pltpu.make_async_copy(loaded.at[v], out_ref.at[:, v], load_sem.at[v]).start()
+        out_ref[:, v] = turned.astype(jnp.bfloat16)
         return carry
 
 
@@ -405,20 +404,23 @@
     def finish(v, carry):
         wait_bytes(recv.at[v, pl.ds(0, n - 1)], send_sem.at[v])
         wait_bytes(done.at[v, pl.ds(0, n - 1)], back_send_sem.at[v])
-        wait_bytes(loaded.at[v], load_sem.at[v])
         return carry
 
     lax.fori_loop(0, VARIABLES, finish, 0)
 
 
 def hand_over(result_ref, out_ref, sem):
-    def piece(v):
-        return pltpu.make_async_copy(result_ref.at[:, v], out_ref.at[:, v], sem.at[v])
-
-    for v in range(VARIABLES):
-        piece(v).start()
-    for v in range(VARIABLES):
-        piece(v).wait()
+    pieces = sem.shape[0]
+    held = result_ref.shape[0] // pieces
+
+    def piece(place):
+        part = pl.ds(place * held, held)
+        return pltpu.make_async_copy(result_ref.at[part], out_ref.at[part], sem.at[place])
+
+    for place in range(pieces):
+        piece(place).start()
+    for place in range(pieces):
+        piece(place).wait()
 
 
 def body(ensemble, observations, precision, valid_count, position, level_kernel, listed_blocks):
@@ -437,7 +439,7 @@
         functools.partial(kernel, n, rows, lead),
         out_shape=jax.ShapeDtypeStruct(shaped.shape, jnp.bfloat16),
         in_specs=[smem, smem, smem, whole, vmem, vmem, vmem],
-        out_specs=whole,
+        out_specs=vmem,
         scratch_shapes=[
             pltpu.VMEM(parts, jnp.bfloat16),
             pltpu.VMEM((VARIABLES, local_members, n, COLUMNS), jnp.bfloat16),
@@ -467,7 +469,7 @@
             sem((3, 3)),
         ],
         compiler_params=pltpu.CompilerParams(
-            collective_id=0, has_side_effects=True, vmem_limit_bytes=56 * 1024 * 1024
+            collective_id=0, has_side_effects=True, vmem_limit_bytes=42 * 1024 * 1024
         ),
     )(
         listed_blocks[0, 0],
@@ -483,8 +485,7 @@
         out_shape=jax.ShapeDtypeStruct(shaped.shape, jnp.bfloat16),
         in_specs=[whole],
         out_specs=whole,
-        scratch_shapes=[sem((VARIABLES,))],
-        compiler_params=pltpu.CompilerParams(vmem_limit_bytes=56 * 1024 * 1024),
+        scratch_shapes=[sem((4,))],
     )(result)
     return result.transpose(0, 2, 1, 3).reshape(ensemble.shape)
 

time: 474 us -> 480 us (1.013)
  local copies, waits for them, and re-layouts: 0 us -> 6.65 us
    unnamed x0 -> x14, local copies, waits for them, and re-layouts: none -> 6.65 us
where the time goes in v5:
time: 480 us
  Pallas kernels  473 us (99%)
  local copies, waits for them, and re-layouts  6.65 us (1%)
    pallas_call x1, Pallas kernels, body(): pl.pallas_call(functools.partial(kernel, n, rows, lead), out_shape=jax.Sh...  281 us
    pallas_call x1, Pallas kernels, body(): pl.pallas_call(hand_over, out_shape=jax.ShapeDtypeStruct(shaped.shape, jn...  192 us

profile of v5, /device:TPU:13, one launch (start us, length us, event | category | flops | bytes accessed | tf_op | source)
XLA Modules:
  0.0 479.7 jit_solution(451619897030619614)
XLA Ops:
  0.0 0.0 copy-start.1
  0.0 0.7 copy-done.1
  0.7 0.0 copy-start.2
  0.7 0.7 copy-done.2
  1.4 0.0 copy-start.3
  1.4 0.7 copy-done.3
  2.0 0.0 copy-start.4
  2.0 0.7 copy-done.4
  2.7 0.0 copy-start.5
  2.7 0.7 copy-done.5
  3.4 0.0 copy-start.6
  3.4 0.7 copy-done.6
  4.0 281.3 %shard_map.73.result_ref = bf16[64,12,4,1024]{3,2,1,0:T(4,128)(2,1)S(1)} custom-call(s32[8]{0:T(128)S(1)} %bitcast.17, s32[2]{0:T(128)S(1)} %bitcast.18, f32[12]{0:T(128)S(1)} %bitcast.19, bf16[64,12,4,1024]{3,2,1,0:T(4,128)(2,1)} %bitcast.20, s32[2,128]{1,0:T(2,128)S(1)} %bitcast.14, f32[2,128]{1,0:T(2,128)S(1)} %bitcast.15, f32[2,128]{1,0:T(2,128)S(1)} %bitcast.16), custom_call_target="tpu_custom_call" | custom-call | tf_op jit(solution)/shard_map/pallas_call | solution.py:438
  285.3 0.0 copy-start
  285.3 2.7 copy-done
  288.0 191.7 %shard_map.74 = bf16[64,12,4,1024]{3,2,1,0:T(4,128)(2,1)} custom-call(bf16[64,12,4,1024]{3,2,1,0:T(4,128)(2,1)} %copy-done), custom_call_target="tpu_custom_call" | custom-call | tf_op jit(solution)/shard_map/pallas_call | solution.py:483
Async XLA Ops:
  0.0 0.7 copy-start.1
  0.7 0.7 copy-start.2
  1.4 0.7 copy-start.3
  2.0 0.7 copy-start.4
  2.7 0.7 copy-start.5
  3.4 0.7 copy-start.6
  285.3 2.7 copy-start

commit v6 on v4

--- a/solution.py
+++ b/solution.py
@@ -411,14 +411,25 @@
     lax.fori_loop(0, VARIABLES, finish, 0)
 
 
-def hand_over(result_ref, out_ref, sem):
-    def piece(v):
-        return pltpu.make_async_copy(result_ref.at[:, v], out_ref.at[:, v], sem.at[v])
-
-    for v in range(VARIABLES):
-        piece(v).start()
-    for v in range(VARIABLES):
-        piece(v).wait()
+def hand_over(result_ref, out_ref, held_ref, load_sem, store_sem):
+    pieces = load_sem.shape[0]
+    length = result_ref.shape[0] // pieces
+
+    def load(place):
+        part = pl.ds(place * length, length)
+        return pltpu.make_async_copy(result_ref.at[part], held_ref.at[part], load_sem.at[place])
+
+    def store(place):
+        part = pl.ds(place * length, length)
+        return pltpu.make_async_copy(held_ref.at[part], out_ref.at[part], store_sem.at[place])
+
+    for place in range(pieces):
+        load(place).start()
+    for place in range(pieces):
+        load(place).wait()
+        store(place).start()
+    for place in range(pieces):
+        store(place).wait()
 
 
 def body(ensemble, observations, precision, valid_count, position, level_kernel, listed_blocks):
@@ -483,7 +494,7 @@
         out_shape=jax.ShapeDtypeStruct(shaped.shape, jnp.bfloat16),
         in_specs=[whole],
         out_specs=whole,
-        scratch_shapes=[sem((VARIABLES,))],
+        scratch_shapes=[pltpu.VMEM(shaped.shape, jnp.bfloat16), sem((8,)), sem((8,))],
         compiler_params=pltpu.CompilerParams(vmem_limit_bytes=56 * 1024 * 1024),
     )(result)
     return result.transpose(0, 2, 1, 3).reshape(ensemble.shape)

time: 474 us -> 288 us (0.61)
  Pallas kernels: 474 us -> 288 us
    pallas_call x1, Pallas kernels: 192 us -> 5.51 us  [body(): pl.pallas_call(hand_over, out_shape=jax.ShapeDtypeStruct(shaped.shape, jn...]
where the time goes in v6:
time: 288 us
  Pallas kernels  288 us (100%)
    pallas_call x1, Pallas kernels, body(): pl.pallas_call(functools.partial(kernel, n, rows, lead), out_shape=jax.Sh...  282 us

profile of v6, /device:TPU:13, one launch (start us, length us, event | category | flops | bytes accessed | tf_op | source)
XLA Modules:
  0.0 287.8 jit_solution(11880874060354238679)
XLA Ops:
  0.0 282.3 %shard_map.73.result_ref = bf16[64,12,4,1024]{3,2,1,0:T(4,128)(2,1)} custom-call(s32[8]{0:T(128)} %bitcast.18, s32[2]{0:T(128)} %bitcast.19, f32[12]{0:T(128)} %bitcast.20, bf16[64,12,4,1024]{3,2,1,0:T(4,128)(2,1)} %bitcast.14, s32[2,128]{1,0:T(2,128)} %bitcast.15, f32[2,128]{1,0:T(2,128)} %bitcast.16, f32[2,128]{1,0:T(2,128)} %bitcast.17), custom_call_target="tpu_custom_call" | custom-call | tf_op jit(solution)/shard_map/pallas_call | solution.py:447
  282.3 5.5 %shard_map.74 = bf16[64,12,4,1024]{3,2,1,0:T(4,128)(2,1)} custom-call(bf16[64,12,4,1024]{3,2,1,0:T(4,128)(2,1)} %shard_map.73.result_ref), custom_call_target="tpu_custom_call" | custom-call | tf_op jit(solution)/shard_map/pallas_call | solution.py:492
